TPU v7x, 32 devices: a whole 2x2x4 slice. The times are simulated.
32 devices in a mesh: img: 8 (over z, y), shot: 4 (over x, core).
Axes of the slice: x: 2, y: 2, z: 4, core: 2. Of those that a mesh axis runs over, the one named last changes fastest.
Arguments:
- shot_green: bfloat16 [2, 3584, 1024], P(None, 'img', 'shot'), may hold values from -6 to 6
- rec_green: bfloat16 [2, 3584, 3584], P(None, 'img'), may hold values from -0.0625 to 0.0625
- model: float32 [3584], P('img'), may hold values from 0.2 to 2
- hadamard_order: int32 [256], replicated, may hold values from 0 to 255, each once
- shot_signs: int32 [1024], P('shot'), may hold values from 0 to 1
Outputs:
- born_data: bfloat16 [2, 3584, 1024], P(None, 'img', 'shot')
Inputs may be any that keep to these rules, and one draw needn't show every extreme that they name: `hadamard_order`: each of 0 to 255 once.
All inputs are finite; a program needn't handle non-finite values.
Results may differ from a plain program's by a relative error of at most 0.0049.
Values may be sent and summed in bfloat16 or wider, within the bound.
A program may use at most 128 MiB of HBM per device.

v0:
```python
import jax
import jax.numpy as jnp
from jax import lax
from jax.sharding import PartitionSpec as P


def parity(values, bit_count):
    result = jnp.zeros_like(values)
    for shift_by in range(bit_count):
        result = jnp.bitwise_xor(result, jnp.bitwise_and(jnp.right_shift(values, shift_by), 1))
    return result


def on_device(shot_green, rec_green, model, hadamard_order, shot_signs):
    shot_local = shot_green.shape[2]
    x_local = shot_green.shape[1]
    blocks = lax.axis_size("shot")
    block_bits = blocks.bit_length() - 1
    columns = jnp.arange(shot_local, dtype=jnp.int32)
    local_code = (
        1
        - 2
        * parity(
            jnp.bitwise_and(hadamard_order[:, None], columns[None, :]), shot_local.bit_length() - 1
        )
    ).astype(jnp.float32)
    signs = (1 - 2 * shot_signs).astype(jnp.float32)
    signed_field = shot_green.astype(jnp.float32) * signs[None, None, :]
    coded = jnp.einsum("pxd,bd->pxb", signed_field, local_code, precision=lax.Precision.HIGHEST)
    my_index = lax.axis_index("shot")
    gathered = lax.all_gather(coded, "shot", axis=2, tiled=True).reshape(
        2, x_local, blocks, shot_local
    )
    block_ids = jnp.arange(blocks, dtype=jnp.int32)
    weights = (1 - 2 * parity(jnp.bitwise_and(my_index, block_ids), block_bits)).astype(jnp.float32)
    encoded = jnp.einsum("pxcb,c->pxb", gathered, weights, precision=lax.Precision.HIGHEST)
    scaled = (model[None, :, None] * encoded * (blocks * shot_local) ** (-0.5)).astype(jnp.bfloat16)
    block_rows = lax.all_gather(scaled, "img", axis=1, tiled=True)
    real_part = jnp.dot(rec_green[0], block_rows[0], preferred_element_type=jnp.float32) - jnp.dot(
        rec_green[1], block_rows[1], preferred_element_type=jnp.float32
    )
    imag_part = jnp.dot(rec_green[0], block_rows[1], preferred_element_type=jnp.float32) + jnp.dot(
        rec_green[1], block_rows[0], preferred_element_type=jnp.float32
    )
    summed = jnp.stack((real_part, imag_part))
    return summed.astype(jnp.bfloat16)


def solution(mesh):
    placed = (P(None, "img", "shot"), P(None, "img", None), P("img"), P(), P("shot"))
    return jax.shard_map(
        on_device, mesh=mesh, in_specs=placed, out_specs=P(None, "img", "shot"), check_vma=False
    )
```

profile of v0, /device:TPU:0, one launch (start us, length us, event | category | flops | bytes accessed | tf_op | source)
XLA Modules:
  0.0 142.5 jit_solution(3556827245080371166)
XLA Ops:
  6.5 0.0 all-gather.3.cloned.1.call-start
  6.5 0.7 subtract_convert_fusion
  7.2 3.1 %fusion.32 = f32[2,448,256]{2,1,0:T(8,128)} fusion(bf16[2,448,256]{2,1,0:T(8,128)(2,1)} %param.5, f32[256]{0:T(256)S(1)} %subtract_convert_fusion, s32[256]{0:T(256)} %param.8), kind=kOutput, calls=%fused_computation.23 | convolution fusion | flops 706871296 | bytes 1378304 | tf_op jit(solution)/shard_map/pxd,bd->pxb/dot_general | solution.py:29
  10.4 0.0 all-gather.3.cloned.1.call-update
  10.4 0.0 all-gather.5.cloned.1.call-start
  10.4 34.3 %all-gather.3.cloned.1.call-done = f32[2,448,1024]{2,1,0:T(8,128)} async-done(((f32[2,448,256]{2,1,0:T(8,128)}), f32[2,448,1024]{2,1,0:T(8,128)}) %all-gather.3.cloned.1.call-update) | async-done | bytes 3670032 | tf_op jit(solution)/shard_map/all_gather | solution.py:31
  44.7 5.3 %reshape.6 = f32[2,448,4,256]{3,2,1,0:T(4,128)} reshape(f32[2,448,1024]{2,1,0:T(8,128)} %all-gather.3.cloned.1.call-done) | data formatting | bytes 7340032 | tf_op jit(solution)/shard_map/reshape | solution.py:31
  50.1 0.0 copy-start
  50.1 8.1 %fusion.74 = f32[1,2,448,256]{3,0,2,1:T(1,128)S(1)} fusion(f32[2,448,4,256]{3,2,1,0:T(4,128)} %reshape.6, s32[]{:T(128)S(6)} %axis_index.12), kind=kOutput, calls=%fused_computation.67 | convolution fusion | flops 11010084 | bytes 4587524 | tf_op jit(solution)/shard_map/pxcb,c->pxb/dot_general | solution.py:36
  58.2 0.0 copy-done
  58.2 0.9 fusion.31
  59.1 0.0 all-gather.5.cloned.1.call-update
  59.1 67.0 %all-gather.5.cloned.1.call-done = bf16[2,3584,256]{2,1,0:T(8,128)(2,1)} async-done(((bf16[2,448,256]{2,1,0:T(8,128)(2,1)}), bf16[2,3584,256]{2,1,0:T(8,128)(2,1)}) %all-gather.5.cloned.1.call-update) | async-done | bytes 3670032 | tf_op jit(solution)/shard_map/all_gather | solution.py:38
  126.1 0.0 copy-start.1
  126.1 0.0 slice-start
  126.1 3.6 %fusion = f32[256,448]{0,1:T(8,128)S(1)} fusion(bf16[2,448,3584]{2,1,0:T(8,128)(2,1)} %param.6, bf16[2,3584,256]{2,1,0:T(8,128)(2,1)} %all-gather.5.cloned.1.call-done), kind=kOutput, calls=%fused_computation | convolution fusion | flops 822083584 | bytes 5505024 | tf_op jit(solution)/shard_map/dot_general | solution.py:39
  129.7 0.0 copy-done.1
  129.7 0.0 slice-start.1
  129.7 3.1 %fusion.2 = f32[256,448]{0,1:T(8,128)S(1)} fusion(bf16[2,448,3584]{2,1,0:T(8,128)(2,1)} %param.6, bf16[2,3584,256]{2,1,0:T(8,128)(2,1)S(1)} %copy-done.1), kind=kOutput, calls=%fused_computation.2 | convolution fusion | flops 822083584 | bytes 5505024 | tf_op jit(solution)/shard_map/dot_general | solution.py:42
  132.8 0.0 slice-done
  132.8 0.0 slice-done.1
  132.9 1.0 fusion.27
  133.9 1.0 fusion.24
  134.9 0.8 pad_maximum_fusion
  (1 shorter events, 0.0 us)
Async XLA Ops:
  6.5 38.2 %all-gather.3.cloned.1.call-start = ((), (), s32[]{:S(2)}) async-start(), calls=%async_computation | async-start | bytes 4587520 | tf_op jit(solution)/shard_map/all_gather | solution.py:31
  10.4 115.7 %all-gather.5.cloned.1.call-start = ((), (), s32[]{:S(2)}) async-start(), calls=%async_computation.1 | async-start | bytes 4128768 | tf_op jit(solution)/shard_map/all_gather | solution.py:38
  50.1 8.1 %copy-start = (f32[448]{0:T(512)S(1)}, f32[448]{0:T(512)}, u32[]{:S(2)}) copy-start(f32[448]{0:T(512)} %param.7) | copy-start | bytes 5380
  126.1 3.6 %copy-start.1 = (bf16[2,3584,256]{2,1,0:T(8,128)(2,1)S(1)}, bf16[2,3584,256]{2,1,0:T(8,128)(2,1)}, u32[]{:S(2)}) copy-start(bf16[2,3584,256]{2,1,0:T(8,128)(2,1)} %all-gather.5.cloned.1.call-done) | copy-start | bytes 11010052
  126.1 6.7 %slice-start = ((s8[6422528]{0:T(1024)(128)(4,1)}), s8[4194304]{0:T(1024)(128)(4,1)S(1)}, s32[]{:S(2)}) async-start(s8[6422528]{0:T(1024)(128)(4,1)} %bitcast.65), calls=%async_computation.2 | async-start | bytes 8388608
  129.7 3.1 %slice-start.1 = ((s8[6422528]{0:T(1024)(128)(4,1)}), s8[2228224]{0:T(1024)(128)(4,1)S(1)}, s32[]{:S(2)}) async-start(s8[6422528]{0:T(1024)(128)(4,1)} %bitcast.65), calls=%async_computation.3 | async-start | bytes 4456448
Sparse Core Ops, SparseCore 0:
  10.5 34.1 all-gather.2
  59.2 66.8 all-gather.4
where the time goes:
time: 143 us
  waiting for transfers between devices  101 us (71%)
  matrix products  19.9 us (14%)
  between operations  13.5 us (9%)
  local copies, waits for them, and re-layouts  5.37 us (4%)
  other arithmetic  2.41 us (2%)
    all_gather x1, waiting for transfers between devices, on_device(): block_rows = lax.all_gather(scaled, 'img', axis=1, tiled=True)  67 us
    all_gather x1, waiting for transfers between devices, on_device(): lax.all_gather(coded, 'shot', axis=2, tiled=True)  34.3 us
    dot_general x1, matrix products, on_device(): jnp.einsum('pxcb,c->pxb', gathered, weights, precision=lax.Precision.HIGH...  8.07 us
    reshape x1, local copies, waits for them, and re-layouts, on_device(): lax.all_gather(coded, 'shot', axis=2, tiled=True)  5.35 us
    dot_general x1, matrix products, on_device(): jnp.dot(rec_green[1], block_rows[1], preferred_element_type=jnp.float32)  3.6 us
    dot_general x1, matrix products, on_device(): jnp.einsum('pxd,bd->pxb', signed_field, local_code, precision=lax.Precisi...  3.14 us
    dot_general x1, matrix products, on_device(): jnp.dot(rec_green[1], block_rows[0], preferred_element_type=jnp.float32)  3.08 us
  transfers between devices with their start and end apart: 2, of which 2 were waited for; matrix products, arithmetic and copies ran while one was open for 0% of the time, Pallas kernels for 0%

commit v1 on v0

v1 whole, which is shorter than its diff:
```python
import functools

import jax
import jax.numpy as jnp
from jax import lax
from jax.experimental import pallas as pl
from jax.experimental.pallas import tpu as pltpu
from jax.sharding import PartitionSpec as P

MESH = pl.DeviceIdType.MESH


def parity(values, bit_count):
    shift_by = 1
    while shift_by < bit_count:
        shift_by *= 2
    while shift_by > 1:
        shift_by //= 2
        values = jnp.bitwise_xor(values, jnp.right_shift(values, shift_by))
    return jnp.bitwise_and(values, 1)


def kernel(
    planes,
    chips,
    chunks,
    relayed,
    green_ref,
    rec_hbm,
    model_ref,
    order_ref,
    signs_ref,
    out_ref,
    raw,
    field,
    rec,
    acc,
    code,
    model_col,
    rec_sem,
    raw_send,
    raw_recv,
    field_send,
    field_recv,
):
    blocks = 2 * chips
    img, shot = lax.axis_index("img"), lax.axis_index("shot")
    z, y = img // 2, img % 2
    chip, core = shot // 2, shot % 2
    other_y = 1 - y
    _, _, part_rows, width = field.shape[1:]
    x_local = chunks * part_rows
    has_up, has_down = z < planes - 1, z > 0
    up = (jnp.minimum(z + 1, planes - 1) * 2 + y, shot)
    down = (jnp.maximum(z - 1, 0) * 2 + y, shot)
    across = (z * 2 + other_y, shot)
    sibling = (img, chip * 2 + 1 - core)

    def far(step):
        return (img, lax.rem(chip + step, chips) * 2 + core)

    barrier = pltpu.get_barrier_semaphore()

    def greet(device):
        pl.semaphore_signal(barrier, inc=1, device_id=device, device_id_type=MESH)

    for step in range(1, chips):
        greet(far(step))
    greet(sibling)
    greet(across)
    pl.when(has_up)(lambda: greet(up))
    pl.when(has_down)(lambda: greet(down))

    rec_copy = pltpu.make_async_copy(rec_hbm, rec, rec_sem)
    rec_copy.start()

    signs = (1 - 2 * signs_ref[...]).astype(jnp.float32)
    for j in range(chunks):
        for p in range(2):
            piece = green_ref[p, j * part_rows : (j + 1) * part_rows, :].astype(jnp.float32)
            raw[shot, j, p] = (piece * signs).astype(jnp.bfloat16)

    pl.semaphore_wait(barrier, chips + 1 + has_up.astype(jnp.int32) + has_down.astype(jnp.int32))

    def send_raw(j, step):
        return pltpu.make_async_remote_copy(
            src_ref=raw.at[shot, j],
            dst_ref=raw.at[shot, j],
            send_sem=raw_send.at[0, step, j],
            recv_sem=raw_recv.at[shot, j],
            device_id=sibling if step == 0 else far(step),
            device_id_type=MESH,
        )

    def pass_raw(j, step):
        owner = lax.rem(chip + step, chips) * 2 + core
        return pltpu.make_async_remote_copy(
            src_ref=raw.at[owner, j],
            dst_ref=raw.at[owner, j],
            send_sem=raw_send.at[1, step, j],
            recv_sem=raw_recv.at[owner, j],
            device_id=sibling,
            device_id_type=MESH,
        )

    def got_raw(owner, j):
        pltpu.make_async_remote_copy(
            src_ref=raw.at[owner, j],
            dst_ref=raw.at[owner, j],
            send_sem=raw_send.at[0, 0, j],
            recv_sem=raw_recv.at[owner, j],
            device_id=sibling,
            device_id_type=MESH,
        ).wait_recv()

    for j in range(chunks):
        for step in range(1, chips):
            send_raw(j, step).start()
        send_raw(j, 0).start()

    d_ids = lax.broadcasted_iota(jnp.int32, (width, width), 0)
    bits = parity(jnp.bitwise_and(order_ref[...], d_ids), width.bit_length() - 1)
    code[...] = (1 - 2 * bits).astype(jnp.float32).astype(jnp.bfloat16)
    row_ids = lax.broadcasted_iota(jnp.int32, (x_local, x_local), 0)
    column_ids = lax.broadcasted_iota(jnp.int32, (x_local, x_local), 1)
    model_col[...] = jnp.sum(
        jnp.where(row_ids == column_ids, model_ref[...], 0.0), axis=1, keepdims=True
    )
    acc[...] = jnp.zeros_like(acc)

    def field_copy(way, block, j):
        return pltpu.make_async_remote_copy(
            src_ref=field.at[block, j],
            dst_ref=field.at[block, j],
            send_sem=field_send.at[way, block, j],
            recv_sem=field_recv.at[block, j],
            device_id=(across, up, down)[way],
            device_id_type=MESH,
        )

    def send(way, block, j):
        field_copy(way, block, j).start()

    def got(block, j):
        field_copy(0, block, j).wait_recv()

    def encode(j, carry):
        for step in range(1, chips):
            got_raw(lax.rem(chip + step, chips) * 2 + core, j)
            pass_raw(j, step).start()
        for step in range(chips):
            got_raw(lax.rem(chip + step, chips) * 2 + 1 - core, j)
        encoded = jnp.zeros((2 * part_rows, width), jnp.float32)
        for c in range(blocks):
            coded = jnp.dot(
                raw[c, j].reshape(2 * part_rows, width),
                code[...],
                preferred_element_type=jnp.float32,
            )
            flip = parity(jnp.bitwise_and(shot, c), blocks.bit_length() - 1)
            encoded += (1 - 2 * flip).astype(jnp.float32) * coded
        rows = pl.multiple_of(j * part_rows, 16)
        model = model_col[pl.ds(rows, part_rows), :]
        for p in range(2):
            scaled = model * encoded[p * part_rows : (p + 1) * part_rows] * (blocks * width) ** (-0.5)
            field[img, j, p] = scaled.astype(jnp.bfloat16)
        send(0, img, j)
        pl.when(has_up)(lambda: send(1, img, j))
        pl.when(has_down)(lambda: send(2, img, j))

        @pl.when(j >= chunks - relayed)
        def _():
            block, k = z * 2 + other_y, j - (chunks - relayed)
            got(block, k)
            pl.when(has_up)(lambda: send(1, block, k))
            pl.when(has_down)(lambda: send(2, block, k))

        return carry

    lax.fori_loop(0, chunks, encode, 0)
    rec_copy.wait()

    def multiply(plane):
        columns = pl.ds(pl.multiple_of(plane * (2 * x_local), 128), 2 * x_local)
        parts = [
            field[pl.ds(plane * 2, 2), :, p].reshape(2 * x_local, width) for p in range(2)
        ]

        def product(q, p):
            return jnp.dot(rec[q, :, columns], parts[p], preferred_element_type=jnp.float32)

        acc[0] += product(0, 0) - product(1, 1)
        acc[1] += product(0, 1) + product(1, 0)

    def at_distance(s, carry):
        ways = ((z - s, z - s >= 0, has_up, 1), (z + s, z + s < planes, has_down, 2))

        def arrive(j, inner):
            for plane, there, onward, way in ways:

                @pl.when(there)
                def _():
                    block = plane * 2 + y
                    got(block, j)
                    pl.when(onward)(lambda: send(way, block, j))
                    pl.when(j >= relayed)(lambda: send(0, block, j))

                @pl.when(there & (j >= chunks - relayed))
                def _():
                    block, k = plane * 2 + other_y, j - (chunks - relayed)
                    got(block, k)
                    pl.when(onward)(lambda: send(way, block, k))

            return inner

        lax.fori_loop(0, chunks, arrive, 0)

        def nearer(which, inner):
            plane = z + (2 * which - 1) * (s - 1)

            @pl.when((plane >= 0) & (plane < planes) & ((s > 1) | (which == 0)))
            def _():
                def wait(j, nothing):
                    got(plane * 2 + other_y, j)
                    return nothing

                lax.fori_loop(relayed, chunks, wait, 0)
                multiply(plane)

            return inner

        lax.fori_loop(0, 2, nearer, 0)
        return carry

    lax.fori_loop(1, planes + 1, at_distance, 0)
    out_ref[...] = acc[...].astype(out_ref.dtype)

    def left_raw(j, carry):
        for step in range(chips):
            send_raw(j, step).wait_send()
        for step in range(1, chips):
            pass_raw(j, step).wait_send()
        return carry

    lax.fori_loop(0, chunks, left_raw, 0)

    def left_field(plane, carry):
        from_below, from_above = plane <= z, plane >= z

        def chunk(j, inner):
            near, opposite = plane * 2 + y, plane * 2 + other_y
            pl.when((j >= relayed) | (plane == z))(lambda: field_copy(0, near, j).wait_send())
            pl.when(from_below & has_up)(lambda: field_copy(1, near, j).wait_send())
            pl.when(from_above & has_down)(lambda: field_copy(2, near, j).wait_send())
            pl.when((j < relayed) & from_below & has_up)(
                lambda: field_copy(1, opposite, j).wait_send()
            )
            pl.when((j < relayed) & from_above & has_down)(
                lambda: field_copy(2, opposite, j).wait_send()
            )
            return inner

        lax.fori_loop(0, chunks, chunk, 0)
        return carry

    lax.fori_loop(0, planes, left_field, 0)


def on_device(shot_green, rec_green, model, hadamard_order, shot_signs):
    _, x_local, width = shot_green.shape
    planes = lax.axis_size("img") // 2
    chips = lax.axis_size("shot") // 2
    chunks = max(n for n in range(1, 9) if x_local % (16 * n) == 0)
    relayed = 1 if chunks > 2 else 0
    part_rows = x_local // chunks
    in_vmem = pl.BlockSpec(memory_space=pltpu.VMEM)
    return pl.pallas_call(
        functools.partial(kernel, planes, chips, chunks, relayed),
        out_shape=jax.ShapeDtypeStruct((2, x_local, width), jnp.bfloat16),
        in_specs=[in_vmem, pl.BlockSpec(memory_space=pl.ANY), in_vmem, in_vmem, in_vmem],
        out_specs=in_vmem,
        scratch_shapes=[
            pltpu.VMEM((2 * chips, chunks, 2, part_rows, width), jnp.bfloat16),
            pltpu.VMEM((2 * planes, chunks, 2, part_rows, width), jnp.bfloat16),
            pltpu.VMEM(rec_green.shape, jnp.bfloat16),
            pltpu.VMEM((2, x_local, width), jnp.float32),
            pltpu.VMEM((width, width), jnp.bfloat16),
            pltpu.VMEM((x_local, 1), jnp.float32),
            pltpu.SemaphoreType.DMA,
            pltpu.SemaphoreType.DMA((2, chips, chunks)),
            pltpu.SemaphoreType.DMA((2 * chips, chunks)),
            pltpu.SemaphoreType.DMA((3, 2 * planes, chunks)),
            pltpu.SemaphoreType.DMA((2 * planes, chunks)),
        ],
        compiler_params=pltpu.CompilerParams(
            collective_id=0, has_side_effects=True, vmem_limit_bytes=48 * 2**20
        ),
        cost_estimate=pl.CostEstimate(
            flops=8 * x_local * rec_green.shape[2] * width,
            bytes_accessed=rec_green.size * 2,
            transcendentals=0,
        ),
    )(
        shot_green,
        rec_green,
        model.reshape(1, x_local),
        hadamard_order.reshape(1, width),
        shot_signs.reshape(1, width),
    )


def solution(mesh):
    placed = (P(None, "img", "shot"), P(None, "img", None), P("img"), P(), P("shot"))
    return jax.shard_map(
        on_device, mesh=mesh, in_specs=placed, out_specs=P(None, "img", "shot"), check_vma=False
    )
```

time: 143 us -> 56.2 us (0.39)
  waiting for transfers between devices: 101 us -> 0 us
  Pallas kernels: 0 us -> 52.2 us
  matrix products: 19.9 us -> 0 us
  between operations: 13.5 us -> 0.01 us
  other arithmetic: 2.41 us -> 0 us
  local copies, waits for them, and re-layouts: 5.37 us -> 3.83 us
    all_gather x2 -> x0, waiting for transfers between devices: 101 us -> none  [the longest x1 67 us: on_device(): block_rows = lax.all_gather(scaled, 'img', axis=1, tiled=True)]
    pallas_call x0 -> x1, Pallas kernels: none -> 52.2 us  [on_device(): pl.pallas_call(functools.partial(kernel, planes, chips, chunks, relayed),...]
    dot_general x6 -> x0, matrix products: 19.9 us -> none  [the longest x1 8.07 us: on_device(): jnp.einsum('pxcb,c->pxb', gathered, weights, precision=lax.Precision.HIGH...]
    reshape x1 -> x0, local copies, waits for them, and re-layouts: 5.35 us -> none  [on_device(): lax.all_gather(coded, 'shot', axis=2, tiled=True)]
    unnamed x8 -> x9, local copies, waits for them, and re-layouts: 0.02 us -> 3.83 us
    convert_element_type x2 -> x0, other arithmetic: 1.6 us -> none  [the longest x1 0.91 us: on_device(): (model[None, :, None] * encoded * (blocks * shot_local) ** (-0.5)).astype...]
  transfers between devices with their start and end apart: 2 -> 0, of which waited for: 2 -> 0; matrix products, arithmetic and copies ran while one was open for 0% -> 0% of each run, Pallas kernels for 0% -> 0%
where the time goes in v1:
time: 56.2 us; the launch traced here: 56 us
  Pallas kernels  52.2 us (93%)
  local copies, waits for them, and re-layouts  3.83 us (7%)
    pallas_call x1, Pallas kernels, on_device(): pl.pallas_call(functools.partial(kernel, planes, chips, chunks, relayed),...  52.2 us
    unnamed x9, local copies, waits for them, and re-layouts  3.83 us

profile of v1, /device:TPU:0, one launch (start us, length us, event | category | flops | bytes accessed | tf_op | source)
XLA Modules:
  0.0 56.0 jit_solution(2954040344120191996)
XLA Ops:
  0.0 0.0 copy-start
  0.0 1.0 %copy-done = bf16[2,448,256]{2,1,0:T(8,128)(2,1)S(1)} copy-done((bf16[2,448,256]{2,1,0:T(8,128)(2,1)S(1)}, bf16[2,448,256]{2,1,0:T(8,128)(2,1)}, u32[]{:S(2)}) %copy-start) | copy-done | bytes 458776
  1.0 0.0 copy-start.1
  1.0 0.7 %copy-done.1 = f32[448]{0:T(512)S(1)} copy-done((f32[448]{0:T(512)S(1)}, f32[448]{0:T(512)}, u32[]{:S(2)}) %copy-start.1) | copy-done | bytes 1816
  1.7 0.0 copy-start.2
  1.7 0.7 %copy-done.2 = s32[256]{0:T(256)S(1)} copy-done((s32[256]{0:T(256)S(1)}, s32[256]{0:T(256)}, u32[]{:S(2)}) %copy-start.2) | copy-done | bytes 1048
  2.4 0.0 copy-start.3
  2.4 0.7 %copy-done.3 = s32[256]{0:T(256)S(1)} copy-done((s32[256]{0:T(256)S(1)}, s32[256]{0:T(256)}, u32[]{:S(2)}) %copy-start.3) | copy-done | bytes 1048
  3.1 52.2 %shard_map.55 = bf16[2,448,256]{2,1,0:T(8,128)(2,1)S(1)} custom-call(bf16[2,448,256]{2,1,0:T(8,128)(2,1)S(1)} %copy-done, bf16[2,448,3584]{2,1,0:T(8,128)(2,1)} %rec_hbm.1, f32[1,448]{1,0:T(1,128)S(1)} %bitcast.3, s32[1,256]{1,0:T(1,128)S(1)} %bitcast.4, s32[1,256]{1,0:T(1,128)S(1)} %bitcast.5), custom_call_target="tpu_custom_call" | custom-call | flops 3288334336 | bytes 6422528 | tf_op jit(solution)/shard_map/pallas_call | solution.py:277
  55.3 0.8 %copy.7 = bf16[2,448,256]{2,1,0:T(8,128)(2,1)} copy(bf16[2,448,256]{2,1,0:T(8,128)(2,1)S(1)} %shard_map.55) | data formatting | bytes 917504
Async XLA Ops:
  0.0 1.0 %copy-start = (bf16[2,448,256]{2,1,0:T(8,128)(2,1)S(1)}, bf16[2,448,256]{2,1,0:T(8,128)(2,1)}, u32[]{:S(2)}) copy-start(bf16[2,448,256]{2,1,0:T(8,128)(2,1)} %green_ref.1) | copy-start | bytes 1376260
  1.0 0.7 %copy-start.1 = (f32[448]{0:T(512)S(1)}, f32[448]{0:T(512)}, u32[]{:S(2)}) copy-start(f32[448]{0:T(512)} %param.7) | copy-start | bytes 5380
  1.7 0.7 %copy-start.2 = (s32[256]{0:T(256)S(1)}, s32[256]{0:T(256)}, u32[]{:S(2)}) copy-start(s32[256]{0:T(256)} %param.8) | copy-start | bytes 3076
  2.4 0.7 %copy-start.3 = (s32[256]{0:T(256)S(1)}, s32[256]{0:T(256)}, u32[]{:S(2)}) copy-start(s32[256]{0:T(256)} %param.9) | copy-start | bytes 3076

commit v2 on v1

--- a/solution.py
+++ b/solution.py
@@ -25,19 +25,23 @@
     chips,
     chunks,
     relayed,
+    green_hbm,
+    rec_hbm,
+    model_hbm,
+    order_hbm,
+    signs_hbm,
+    out_ref,
     green_ref,
-    rec_hbm,
     model_ref,
     order_ref,
     signs_ref,
-    out_ref,
     raw,
     field,
     rec,
     acc,
     code,
     model_col,
-    rec_sem,
+    load_sem,
     raw_send,
     raw_recv,
     field_send,
@@ -59,6 +63,19 @@
     def far(step):
         return (img, lax.rem(chip + step, chips) * 2 + core)
 
+    loads = [
+        pltpu.make_async_copy(source, target, load_sem.at[n])
+        for n, (source, target) in enumerate(
+            (
+                (signs_hbm, signs_ref),
+                (green_hbm, green_ref),
+                (order_hbm, order_ref),
+                (model_hbm, model_ref),
+                (rec_hbm, rec),
+            )
+        )
+    ]
+
     barrier = pltpu.get_barrier_semaphore()
 
     def greet(device):
@@ -71,8 +88,10 @@
     pl.when(has_up)(lambda: greet(up))
     pl.when(has_down)(lambda: greet(down))
 
-    rec_copy = pltpu.make_async_copy(rec_hbm, rec, rec_sem)
-    rec_copy.start()
+    for load in loads:
+        load.start()
+    for load in loads[:2]:
+        load.wait()
 
     signs = (1 - 2 * signs_ref[...]).astype(jnp.float32)
     for j in range(chunks):
@@ -86,7 +105,7 @@
         return pltpu.make_async_remote_copy(
             src_ref=raw.at[shot, j],
             dst_ref=raw.at[shot, j],
-            send_sem=raw_send.at[0, step, j],
+            send_sem=raw_send.at[0, step],
             recv_sem=raw_recv.at[shot, j],
             device_id=sibling if step == 0 else far(step),
             device_id_type=MESH,
@@ -97,7 +116,7 @@
         return pltpu.make_async_remote_copy(
             src_ref=raw.at[owner, j],
             dst_ref=raw.at[owner, j],
-            send_sem=raw_send.at[1, step, j],
+            send_sem=raw_send.at[1, step],
             recv_sem=raw_recv.at[owner, j],
             device_id=sibling,
             device_id_type=MESH,
@@ -107,7 +126,7 @@
         pltpu.make_async_remote_copy(
             src_ref=raw.at[owner, j],
             dst_ref=raw.at[owner, j],
-            send_sem=raw_send.at[0, 0, j],
+            send_sem=raw_send.at[0, 0],
             recv_sem=raw_recv.at[owner, j],
             device_id=sibling,
             device_id_type=MESH,
@@ -117,6 +136,9 @@
         for step in range(1, chips):
             send_raw(j, step).start()
         send_raw(j, 0).start()
+
+    for load in loads[2:4]:
+        load.wait()
 
     d_ids = lax.broadcasted_iota(jnp.int32, (width, width), 0)
     bits = parity(jnp.bitwise_and(order_ref[...], d_ids), width.bit_length() - 1)
@@ -132,7 +154,7 @@
         return pltpu.make_async_remote_copy(
             src_ref=field.at[block, j],
             dst_ref=field.at[block, j],
-            send_sem=field_send.at[way, block, j],
+            send_sem=field_send.at[way, block],
             recv_sem=field_recv.at[block, j],
             device_id=(across, up, down)[way],
             device_id_type=MESH,
@@ -144,19 +166,25 @@
     def got(block, j):
         field_copy(0, block, j).wait_recv()
 
-    def encode(j, carry):
+    def relay_raw(j):
         for step in range(1, chips):
             got_raw(lax.rem(chip + step, chips) * 2 + core, j)
             pass_raw(j, step).start()
+
+    relay_raw(0)
+
+    def encode(j, carry):
+        pl.when(j + 1 < chunks)(lambda: relay_raw(j + 1))
         for step in range(chips):
             got_raw(lax.rem(chip + step, chips) * 2 + 1 - core, j)
+        all_coded = jnp.dot(
+            raw[:, j].reshape(blocks * 2 * part_rows, width),
+            code[...],
+            preferred_element_type=jnp.float32,
+        )
         encoded = jnp.zeros((2 * part_rows, width), jnp.float32)
         for c in range(blocks):
-            coded = jnp.dot(
-                raw[c, j].reshape(2 * part_rows, width),
-                code[...],
-                preferred_element_type=jnp.float32,
-            )
+            coded = all_coded[c * 2 * part_rows : (c + 1) * 2 * part_rows]
             flip = parity(jnp.bitwise_and(shot, c), blocks.bit_length() - 1)
             encoded += (1 - 2 * flip).astype(jnp.float32) * coded
         rows = pl.multiple_of(j * part_rows, 16)
@@ -178,7 +206,7 @@
         return carry
 
     lax.fori_loop(0, chunks, encode, 0)
-    rec_copy.wait()
+    loads[4].wait()
 
     def multiply(plane):
         columns = pl.ds(pl.multiple_of(plane * (2 * x_local), 128), 2 * x_local)
@@ -191,6 +219,42 @@
 
         acc[0] += product(0, 0) - product(1, 1)
         acc[1] += product(0, 1) + product(1, 0)
+
+    def left(buffer, semaphore):
+        pltpu.make_async_remote_copy(
+            src_ref=buffer,
+            dst_ref=buffer,
+            send_sem=semaphore,
+            recv_sem=field_recv.at[0, 0],
+            device_id=sibling,
+            device_id_type=MESH,
+        ).wait_send()
+
+    def left_raw():
+        for step in range(chips):
+            left(raw.at[shot], raw_send.at[0, step])
+        for step in range(1, chips):
+            left(raw.at[lax.rem(chip + step, chips) * 2 + core], raw_send.at[1, step])
+
+    def left_field(plane, carry):
+        from_below, from_above = plane <= z, plane >= z
+        near, opposite = plane * 2 + y, plane * 2 + other_y
+        if relayed:
+            pl.when(plane == z)(lambda: left(field.at[near], field_send.at[0, near]))
+            pl.when(plane != z)(
+                lambda: left(field.at[near, pl.ds(relayed, chunks - relayed)], field_send.at[0, near])
+            )
+        else:
+            left(field.at[near], field_send.at[0, near])
+        for goes, way in ((from_below & has_up, 1), (from_above & has_down, 2)):
+
+            @pl.when(goes)
+            def _():
+                left(field.at[near], field_send.at[way, near])
+                if relayed:
+                    left(field.at[opposite, pl.ds(0, relayed)], field_send.at[way, opposite])
+
+        return carry
 
     def at_distance(s, carry):
         ways = ((z - s, z - s >= 0, has_up, 1), (z + s, z + s < planes, has_down, 2))
@@ -215,6 +279,11 @@
 
         lax.fori_loop(0, chunks, arrive, 0)
 
+        @pl.when(s == planes)
+        def _():
+            left_raw()
+            lax.fori_loop(0, planes, left_field, 0)
+
         def nearer(which, inner):
             plane = z + (2 * which - 1) * (s - 1)
 
@@ -234,36 +303,6 @@
 
     lax.fori_loop(1, planes + 1, at_distance, 0)
     out_ref[...] = acc[...].astype(out_ref.dtype)
-
-    def left_raw(j, carry):
-        for step in range(chips):
-            send_raw(j, step).wait_send()
-        for step in range(1, chips):
-            pass_raw(j, step).wait_send()
-        return carry
-
-    lax.fori_loop(0, chunks, left_raw, 0)
-
-    def left_field(plane, carry):
-        from_below, from_above = plane <= z, plane >= z
-
-        def chunk(j, inner):
-            near, opposite = plane * 2 + y, plane * 2 + other_y
-            pl.when((j >= relayed) | (plane == z))(lambda: field_copy(0, near, j).wait_send())
-            pl.when(from_below & has_up)(lambda: field_copy(1, near, j).wait_send())
-            pl.when(from_above & has_down)(lambda: field_copy(2, near, j).wait_send())
-            pl.when((j < relayed) & from_below & has_up)(
-                lambda: field_copy(1, opposite, j).wait_send()
-            )
-            pl.when((j < relayed) & from_above & has_down)(
-                lambda: field_copy(2, opposite, j).wait_send()
-            )
-            return inner
-
-        lax.fori_loop(0, chunks, chunk, 0)
-        return carry
-
-    lax.fori_loop(0, planes, left_field, 0)
 
 
 def on_device(shot_green, rec_green, model, hadamard_order, shot_signs):
@@ -273,23 +312,27 @@
     chunks = max(n for n in range(1, 9) if x_local % (16 * n) == 0)
     relayed = 1 if chunks > 2 else 0
     part_rows = x_local // chunks
-    in_vmem = pl.BlockSpec(memory_space=pltpu.VMEM)
+    in_hbm = pl.BlockSpec(memory_space=pltpu.HBM)
     return pl.pallas_call(
         functools.partial(kernel, planes, chips, chunks, relayed),
         out_shape=jax.ShapeDtypeStruct((2, x_local, width), jnp.bfloat16),
-        in_specs=[in_vmem, pl.BlockSpec(memory_space=pl.ANY), in_vmem, in_vmem, in_vmem],
-        out_specs=in_vmem,
+        in_specs=[in_hbm] * 5,
+        out_specs=pl.BlockSpec(memory_space=pltpu.VMEM),
         scratch_shapes=[
+            pltpu.VMEM(shot_green.shape, jnp.bfloat16),
+            pltpu.VMEM((1, x_local), jnp.float32),
+            pltpu.VMEM((1, width), jnp.int32),
+            pltpu.VMEM((1, width), jnp.int32),
             pltpu.VMEM((2 * chips, chunks, 2, part_rows, width), jnp.bfloat16),
             pltpu.VMEM((2 * planes, chunks, 2, part_rows, width), jnp.bfloat16),
             pltpu.VMEM(rec_green.shape, jnp.bfloat16),
             pltpu.VMEM((2, x_local, width), jnp.float32),
             pltpu.VMEM((width, width), jnp.bfloat16),
             pltpu.VMEM((x_local, 1), jnp.float32),
-            pltpu.SemaphoreType.DMA,
-            pltpu.SemaphoreType.DMA((2, chips, chunks)),
+            pltpu.SemaphoreType.DMA((5,)),
+            pltpu.SemaphoreType.DMA((2, chips)),
             pltpu.SemaphoreType.DMA((2 * chips, chunks)),
-            pltpu.SemaphoreType.DMA((3, 2 * planes, chunks)),
+            pltpu.SemaphoreType.DMA((3, 2 * planes)),
             pltpu.SemaphoreType.DMA((2 * planes, chunks)),
         ],
         compiler_params=pltpu.CompilerParams(

time: 56.2 us -> 54.1 us (0.963)
  Pallas kernels: 52.2 us -> 50.1 us
    pallas_call x1, Pallas kernels: 52.2 us -> 50.1 us  [on_device(): pl.pallas_call(functools.partial(kernel, planes, chips, chunks, relayed),...]
where the time goes in v2:
time: 54.1 us; the launch traced here: 53.9 us
  Pallas kernels  50.1 us (93%)
  local copies, waits for them, and re-layouts  3.83 us (7%)
    pallas_call x1, Pallas kernels, on_device(): pl.pallas_call(functools.partial(kernel, planes, chips, chunks, relayed),...  50.1 us
    unnamed x9, local copies, waits for them, and re-layouts  3.83 us

profile of v2, /device:TPU:0, one launch (start us, length us, event | category | flops | bytes accessed | tf_op | source)
XLA Modules:
  0.0 53.9 jit_solution(11532919571394204758)
XLA Ops:
  0.0 0.0 copy-start
  0.0 1.0 %copy-done = bf16[2,448,256]{2,1,0:T(8,128)(2,1)S(1)} copy-done((bf16[2,448,256]{2,1,0:T(8,128)(2,1)S(1)}, bf16[2,448,256]{2,1,0:T(8,128)(2,1)}, u32[]{:S(2)}) %copy-start) | copy-done | bytes 458776
  1.0 0.0 copy-start.1
  1.0 0.7 %copy-done.1 = f32[448]{0:T(512)S(1)} copy-done((f32[448]{0:T(512)S(1)}, f32[448]{0:T(512)}, u32[]{:S(2)}) %copy-start.1) | copy-done | bytes 1816
  1.7 0.0 copy-start.2
  1.7 0.7 %copy-done.2 = s32[256]{0:T(256)S(1)} copy-done((s32[256]{0:T(256)S(1)}, s32[256]{0:T(256)}, u32[]{:S(2)}) %copy-start.2) | copy-done | bytes 1048
  2.4 0.0 copy-start.3
  2.4 0.7 %copy-done.3 = s32[256]{0:T(256)S(1)} copy-done((s32[256]{0:T(256)S(1)}, s32[256]{0:T(256)}, u32[]{:S(2)}) %copy-start.3) | copy-done | bytes 1048
  3.1 50.1 %shard_map.55 = bf16[2,448,256]{2,1,0:T(8,128)(2,1)S(1)} custom-call(bf16[2,448,256]{2,1,0:T(8,128)(2,1)S(1)} %copy-done, bf16[2,448,3584]{2,1,0:T(8,128)(2,1)} %rec_hbm.1, f32[1,448]{1,0:T(1,128)S(1)} %bitcast.3, s32[1,256]{1,0:T(1,128)S(1)} %bitcast.4, s32[1,256]{1,0:T(1,128)S(1)} %bitcast.5), custom_call_target="tpu_custom_call" | custom-call | flops 3288334336 | bytes 6422528 | tf_op jit(solution)/shard_map/pallas_call | solution.py:316
  53.1 0.8 %copy.7 = bf16[2,448,256]{2,1,0:T(8,128)(2,1)} copy(bf16[2,448,256]{2,1,0:T(8,128)(2,1)S(1)} %shard_map.55) | data formatting | bytes 917504
Async XLA Ops:
  0.0 1.0 %copy-start = (bf16[2,448,256]{2,1,0:T(8,128)(2,1)S(1)}, bf16[2,448,256]{2,1,0:T(8,128)(2,1)}, u32[]{:S(2)}) copy-start(bf16[2,448,256]{2,1,0:T(8,128)(2,1)} %green_hbm.1) | copy-start | bytes 1376260
  1.0 0.7 %copy-start.1 = (f32[448]{0:T(512)S(1)}, f32[448]{0:T(512)}, u32[]{:S(2)}) copy-start(f32[448]{0:T(512)} %param.7) | copy-start | bytes 5380
  1.7 0.7 %copy-start.2 = (s32[256]{0:T(256)S(1)}, s32[256]{0:T(256)}, u32[]{:S(2)}) copy-start(s32[256]{0:T(256)} %param.8) | copy-start | bytes 3076
  2.4 0.7 %copy-start.3 = (s32[256]{0:T(256)S(1)}, s32[256]{0:T(256)}, u32[]{:S(2)}) copy-start(s32[256]{0:T(256)} %param.9) | copy-start | bytes 3076

commit v3 on v2

--- a/solution.py
+++ b/solution.py
@@ -46,6 +46,7 @@
     raw_recv,
     field_send,
     field_recv,
+    across_recv,
 ):
     blocks = 2 * chips
     img, shot = lax.axis_index("img"), lax.axis_index("shot")
@@ -160,6 +161,16 @@
             device_id_type=MESH,
         )
 
+    def send_across(block, j):
+        pltpu.make_async_remote_copy(
+            src_ref=field.at[block, j],
+            dst_ref=field.at[block, j],
+            send_sem=field_send.at[0, block],
+            recv_sem=across_recv.at[block],
+            device_id=across,
+            device_id_type=MESH,
+        ).start()
+
     def send(way, block, j):
         field_copy(way, block, j).start()
 
@@ -192,7 +203,8 @@
         for p in range(2):
             scaled = model * encoded[p * part_rows : (p + 1) * part_rows] * (blocks * width) ** (-0.5)
             field[img, j, p] = scaled.astype(jnp.bfloat16)
-        send(0, img, j)
+        pl.when(j < relayed)(lambda: send(0, img, j))
+        pl.when(j >= relayed)(lambda: send_across(img, j))
         pl.when(has_up)(lambda: send(1, img, j))
         pl.when(has_down)(lambda: send(2, img, j))
 
@@ -267,7 +279,7 @@
                     block = plane * 2 + y
                     got(block, j)
                     pl.when(onward)(lambda: send(way, block, j))
-                    pl.when(j >= relayed)(lambda: send(0, block, j))
+                    pl.when(j >= relayed)(lambda: send_across(block, j))
 
                 @pl.when(there & (j >= chunks - relayed))
                 def _():
@@ -289,11 +301,16 @@
 
             @pl.when((plane >= 0) & (plane < planes) & ((s > 1) | (which == 0)))
             def _():
-                def wait(j, nothing):
-                    got(plane * 2 + other_y, j)
-                    return nothing
-
-                lax.fori_loop(relayed, chunks, wait, 0)
+                block = plane * 2 + other_y
+                rest = field.at[block, pl.ds(relayed, chunks - relayed)]
+                pltpu.make_async_remote_copy(
+                    src_ref=rest,
+                    dst_ref=rest,
+                    send_sem=field_send.at[0, block],
+                    recv_sem=across_recv.at[block],
+                    device_id=across,
+                    device_id_type=MESH,
+                ).wait_recv()
                 multiply(plane)
 
             return inner
@@ -334,6 +351,7 @@
             pltpu.SemaphoreType.DMA((2 * chips, chunks)),
             pltpu.SemaphoreType.DMA((3, 2 * planes)),
             pltpu.SemaphoreType.DMA((2 * planes, chunks)),
+            pltpu.SemaphoreType.DMA((2 * planes,)),
         ],
         compiler_params=pltpu.CompilerParams(
             collective_id=0, has_side_effects=True, vmem_limit_bytes=48 * 2**20

time: 54.1 us -> 54.2 us (level)
  no operation moved by 1% of the time
where the time goes in v3:
time: 54.2 us; the launch traced here: 54 us
  Pallas kernels  50.1 us (92%)
  local copies, waits for them, and re-layouts  3.83 us (7%)
    pallas_call x1, Pallas kernels, on_device(): pl.pallas_call(functools.partial(kernel, planes, chips, chunks, relayed),...  50.1 us
    unnamed x9, local copies, waits for them, and re-layouts  3.83 us

profile of v3, /device:TPU:0, one launch (start us, length us, event | category | flops | bytes accessed | tf_op | source)
XLA Modules:
  0.0 54.0 jit_solution(8893519372104758960)
XLA Ops:
  0.0 0.0 copy-start
  0.0 1.0 %copy-done = bf16[2,448,256]{2,1,0:T(8,128)(2,1)S(1)} copy-done((bf16[2,448,256]{2,1,0:T(8,128)(2,1)S(1)}, bf16[2,448,256]{2,1,0:T(8,128)(2,1)}, u32[]{:S(2)}) %copy-start) | copy-done | bytes 458776
  1.0 0.0 copy-start.1
  1.0 0.7 %copy-done.1 = f32[448]{0:T(512)S(1)} copy-done((f32[448]{0:T(512)S(1)}, f32[448]{0:T(512)}, u32[]{:S(2)}) %copy-start.1) | copy-done | bytes 1816
  1.7 0.0 copy-start.2
  1.7 0.7 %copy-done.2 = s32[256]{0:T(256)S(1)} copy-done((s32[256]{0:T(256)S(1)}, s32[256]{0:T(256)}, u32[]{:S(2)}) %copy-start.2) | copy-done | bytes 1048
  2.4 0.0 copy-start.3
  2.4 0.7 %copy-done.3 = s32[256]{0:T(256)S(1)} copy-done((s32[256]{0:T(256)S(1)}, s32[256]{0:T(256)}, u32[]{:S(2)}) %copy-start.3) | copy-done | bytes 1048
  3.1 50.1 %shard_map.55 = bf16[2,448,256]{2,1,0:T(8,128)(2,1)S(1)} custom-call(bf16[2,448,256]{2,1,0:T(8,128)(2,1)S(1)} %copy-done, bf16[2,448,3584]{2,1,0:T(8,128)(2,1)} %rec_hbm.1, f32[1,448]{1,0:T(1,128)S(1)} %bitcast.3, s32[1,256]{1,0:T(1,128)S(1)} %bitcast.4, s32[1,256]{1,0:T(1,128)S(1)} %bitcast.5), custom_call_target="tpu_custom_call" | custom-call | flops 3288334336 | bytes 6422528 | tf_op jit(solution)/shard_map/pallas_call | solution.py:333
  53.2 0.8 %copy.7 = bf16[2,448,256]{2,1,0:T(8,128)(2,1)} copy(bf16[2,448,256]{2,1,0:T(8,128)(2,1)S(1)} %shard_map.55) | data formatting | bytes 917504
Async XLA Ops:
  0.0 1.0 %copy-start = (bf16[2,448,256]{2,1,0:T(8,128)(2,1)S(1)}, bf16[2,448,256]{2,1,0:T(8,128)(2,1)}, u32[]{:S(2)}) copy-start(bf16[2,448,256]{2,1,0:T(8,128)(2,1)} %green_hbm.1) | copy-start | bytes 1376260
  1.0 0.7 %copy-start.1 = (f32[448]{0:T(512)S(1)}, f32[448]{0:T(512)}, u32[]{:S(2)}) copy-start(f32[448]{0:T(512)} %param.7) | copy-start | bytes 5380
  1.7 0.7 %copy-start.2 = (s32[256]{0:T(256)S(1)}, s32[256]{0:T(256)}, u32[]{:S(2)}) copy-start(s32[256]{0:T(256)} %param.8) | copy-start | bytes 3076
  2.4 0.7 %copy-start.3 = (s32[256]{0:T(256)S(1)}, s32[256]{0:T(256)}, u32[]{:S(2)}) copy-start(s32[256]{0:T(256)} %param.9) | copy-start | bytes 3076
